TPU v7x, 32 devices: a whole 2x2x4 slice. The times are simulated.
32 devices in a mesh: crop: 4 (over x, core), seq: 8 (over z, y).
Axes of the slice: x: 2, y: 2, z: 4, core: 2. Of those that a mesh axis runs over, the one named last changes fastest.
Arguments:
- queries: bfloat16 [4096, 2048], P(('crop', 'seq')), parts along dimension 0, may hold values from -13 to 13
- keys: bfloat16 [4096, 2048], P(('crop', 'seq')), parts along dimension 0, may hold values from -6 to 6
- values: bfloat16 [4096, 2048], P(('crop', 'seq')), parts along dimension 0, may hold values from -6 to 6
- proj_weight: bfloat16 [2048, 256], replicated, may hold values from -0.125 to 0.125
- norm_gain: float32 [256], replicated, may hold values from 0.1 to 1.9
- conv_weight: bfloat16 [9, 256, 256], replicated, may hold values from -0.125 to 0.125
- conv_bias: float32 [256], replicated, may hold values from -3 to 3
- class_weight: bfloat16 [9, 16, 256], replicated, may hold values from -4.5 to 4.5
- class_bias: float32 [16], replicated, may hold values from -4 to 4
- labels: int32 [256, 256], P(('crop', 'seq')), parts along dimension 0, may hold values from 0 to 15
Outputs:
- logits: float32 [16, 256, 256], P(None, ('crop', 'seq')), parts along dimension 1
- pixel_loss: float32 [256, 256], P(('crop', 'seq')), parts along dimension 0
- loss: float32 [4], P('crop'), parts along dimension 0
There are 4 independent parts, one for each index of `crop`. A program takes and returns all parts, laid end to end along the dimension named above; an argument that names none is the same for every part. Nothing has to cross between parts.
All inputs are finite; a program needn't handle non-finite values.
Results may differ from a plain program's by a relative error of at most 0.0085.
The roundings to bfloat16 on the way count: a program that leaves them out, or rounds other values in their place, can miss the bound.
Values may be sent and summed in bfloat16 or wider, within the bound.
A program may use at most 64 MiB of HBM per device.

v0:
```python
import math

import jax
import jax.numpy as jnp
from jax import lax
from jax.sharding import PartitionSpec as P

HEADS = 16
HEAD_DIM = 128
UPSCALE = 4
GRID_COLS = 64


EPSILON = 1e-05


def extended_2(block, sides, width):
    for axis, dim in sides:
        count = lax.axis_size(axis)
        forward = [(i, i + 1) for i in range(count - 1)]
        backward = [(target, source) for source, target in forward]
        low = lax.ppermute(
            lax.slice_in_dim(block, block.shape[dim] - width, None, axis=dim), axis, forward
        )
        high = lax.ppermute(lax.slice_in_dim(block, 0, width, axis=dim), axis, backward)
        block = jnp.concatenate([low, block, high], axis=dim)
    return block


def rotate(packed, row_ids, col_ids):
    count_rows = packed.shape[0]
    head_rows = packed.reshape(count_rows, HEADS, HEAD_DIM).astype(jnp.float32)
    quarter = HEAD_DIM // 4
    omegas = jnp.power(jnp.float32(100.0), -jnp.arange(quarter, dtype=jnp.float32) / quarter)
    pieces = []
    for coords, offset in ((row_ids, 0), (col_ids, 2 * quarter)):
        angles = coords.astype(jnp.float32)[:, None, None] * omegas[None, None, :]
        cosine = jnp.cos(angles)
        sine_part = jnp.sin(angles)
        first_half = head_rows[:, :, offset : offset + quarter]
        second_half = head_rows[:, :, offset + quarter : offset + 2 * quarter]
        pieces.append(first_half * cosine - second_half * sine_part)
        pieces.append(second_half * cosine + first_half * sine_part)
    return (
        jnp.concatenate(pieces, axis=2).reshape(count_rows, HEADS * HEAD_DIM).astype(jnp.bfloat16)
    )


def attend(queries, keys, values):
    total_rows = queries.shape[0]
    block = math.gcd(512, total_rows)
    scale = queries.shape[2] ** (-0.5)

    def one_block(query_block):
        scores = (
            jnp.einsum("qhd,khd->hqk", query_block, keys, preferred_element_type=jnp.float32)
            * scale
        )
        highest = jnp.max(scores, axis=2, keepdims=True)
        exponent = jnp.exp(scores - highest)
        weights = (exponent / jnp.sum(exponent, axis=2, keepdims=True)).astype(jnp.bfloat16)
        mixed = jnp.einsum("hqk,khd->qhd", weights, values, preferred_element_type=jnp.float32)
        return mixed.astype(jnp.bfloat16)

    blocked = queries.reshape(total_rows // block, block, queries.shape[1], queries.shape[2])
    return lax.map(one_block, blocked).reshape(queries.shape)


def normalize(features, gain):
    center = jnp.mean(features, axis=-1, keepdims=True)
    spread = jnp.mean((features - center) ** 2, axis=-1, keepdims=True)
    return (features - center) / jnp.sqrt(spread + EPSILON) * gain


def convolve(padded, weight):
    out_rows = padded.shape[0] - 2
    out_cols = padded.shape[1] - 2
    summed = jnp.zeros((out_rows * out_cols, weight.shape[2]), jnp.float32)
    for tap_index in range(9):
        tap_row, tap_col = (tap_index // 3, tap_index % 3)
        window = padded[tap_row : tap_row + out_rows, tap_col : tap_col + out_cols].reshape(
            -1, padded.shape[2]
        )
        summed = summed + jnp.dot(window, weight[tap_index], preferred_element_type=jnp.float32)
    return summed.reshape(out_rows, out_cols, weight.shape[2])


def classify(padded, class_weight):
    out_rows = padded.shape[0] - 2
    out_cols = padded.shape[1] - 2
    summed = jnp.zeros((class_weight.shape[1], out_rows * out_cols), jnp.float32)
    for tap_index in range(9):
        tap_row, tap_col = (tap_index // 3, tap_index % 3)
        window = padded[tap_row : tap_row + out_rows, tap_col : tap_col + out_cols].reshape(
            -1, padded.shape[2]
        )
        summed = summed + lax.dot_general(
            class_weight[tap_index],
            window,
            (((1,), (1,)), ((), ())),
            preferred_element_type=jnp.float32,
        )
    return summed.reshape(class_weight.shape[1], out_rows, out_cols)


def pixel_losses(logits, labels):
    highest = jnp.max(logits, axis=0)
    log_total = highest + jnp.log(jnp.sum(jnp.exp(logits - highest[None]), axis=0))
    class_ids = jnp.arange(logits.shape[0], dtype=jnp.int32)[:, None, None]
    picked = jnp.sum(jnp.where(class_ids == labels[None], logits, jnp.zeros_like(logits)), axis=0)
    return log_total - picked


def to_heads(query_send, key_grouped, value_grouped, split):
    key_send = jnp.repeat(key_grouped, split, axis=1)
    value_send = jnp.repeat(value_grouped, split, axis=1)
    return (
        lax.all_to_all(query_send, "seq", split_axis=1, concat_axis=0, tiled=True),
        lax.all_to_all(key_send, "seq", split_axis=1, concat_axis=0, tiled=True),
        lax.all_to_all(value_send, "seq", split_axis=1, concat_axis=0, tiled=True),
    )


def body(
    queries,
    keys,
    values,
    proj_weight,
    norm_gain,
    conv_weight,
    conv_bias,
    class_weight,
    class_bias,
    labels,
):
    devices = lax.axis_size("seq")
    place = lax.axis_index("seq")
    local_tokens = queries.shape[0]
    strip = local_tokens // GRID_COLS
    positions = jnp.arange(local_tokens, dtype=jnp.int32)
    row_ids = place * strip + positions // GRID_COLS
    col_ids = positions % GRID_COLS
    rotated_queries = rotate(queries, row_ids, col_ids)
    rotated_keys = rotate(keys, row_ids, col_ids)
    if devices >= HEADS:
        per_device = 1
        split = devices // HEADS
    else:
        per_device = HEADS // devices
        split = 1
    groups = HEADS // per_device
    width = per_device * HEAD_DIM
    part_rows = local_tokens // split
    query_send = (
        rotated_queries.reshape(split, part_rows, groups, width)
        .transpose(1, 2, 0, 3)
        .reshape(part_rows, devices, width)
    )
    key_grouped = rotated_keys.reshape(local_tokens, groups, width)
    value_grouped = values.reshape(local_tokens, groups, width)
    query_recv, key_recv, value_recv = to_heads(query_send, key_grouped, value_grouped, split)
    attended = attend(
        query_recv.reshape(-1, per_device, HEAD_DIM),
        key_recv.reshape(-1, per_device, HEAD_DIM),
        value_recv.reshape(-1, per_device, HEAD_DIM),
    )
    outgoing = attended.reshape(devices, part_rows, width)
    returned = lax.all_to_all(outgoing, "seq", split_axis=0, concat_axis=0, tiled=True)
    mixed = (
        returned.reshape(groups, split, part_rows, width)
        .transpose(1, 2, 0, 3)
        .reshape(local_tokens, HEADS * HEAD_DIM)
    )
    features = jnp.dot(mixed, proj_weight, preferred_element_type=jnp.float32)
    activated = jax.nn.gelu(normalize(features, norm_gain), approximate=False).astype(jnp.bfloat16)
    activated = activated.reshape(strip, GRID_COLS, -1)
    extended = extended_2(activated, (("seq", 0),), 2)
    padded = jnp.pad(extended, ((0, 0), (1, 1), (0, 0)))
    hidden = jax.nn.gelu(convolve(padded, conv_weight) + conv_bias, approximate=False)
    grid_rows = place * strip - 1 + jnp.arange(strip + 2, dtype=jnp.int32)
    inside = (grid_rows >= 0) & (grid_rows < strip * devices)
    hidden_ext = jnp.where(inside[:, None, None], hidden, jnp.zeros_like(hidden)).astype(
        jnp.bfloat16
    )
    upsampled = jnp.repeat(hidden_ext, UPSCALE, axis=0)[
        UPSCALE - 1 : UPSCALE - 1 + UPSCALE * strip + 2
    ]
    upsampled = jnp.repeat(upsampled, UPSCALE, axis=1)
    logits = (
        classify(jnp.pad(upsampled, ((0, 0), (1, 1), (0, 0))), class_weight)
        + class_bias[:, None, None]
    )
    losses = pixel_losses(logits, labels)
    summed_loss = lax.psum(jnp.sum(losses), "seq")
    loss = (summed_loss / (losses.shape[0] * losses.shape[1] * devices)).reshape(1)
    return (logits, losses, loss)


def solution(mesh):
    in_specs = (
        P(("crop", "seq"), None),
        P(("crop", "seq"), None),
        P(("crop", "seq"), None),
        P(),
        P(),
        P(),
        P(),
        P(),
        P(),
        P(("crop", "seq"), None),
    )
    out_specs = (P(None, ("crop", "seq"), None), P(("crop", "seq"), None), P("crop"))
    return jax.shard_map(body, mesh=mesh, in_specs=in_specs, out_specs=out_specs, check_vma=False)
```

profile of v0, /device:TPU:0, one launch (start us, length us, event | category | flops | bytes accessed | tf_op | source)
XLA Modules:
  0.0 155.0 jit_solution(18244871583844804303)
XLA Ops:
  0.7 1.3 copy.31
  2.0 0.2 multiply_cosine_fusion.1
  2.4 0.9 pad_maximum_fusion.1
  3.2 7.3 %all-to-all-start.1 = ((bf16[128,8,256]{0,2,1:T(8,128)(2,1)}), bf16[128,8,256]{0,2,1:T(8,128)(2,1)S(1)}, u32[]{:S(2)}, u32[]{:S(2)}) async-start(bf16[128,8,256]{0,2,1:T(8,128)(2,1)} %bitcast.8), calls=%async_computation.1 | async-start | bytes 1048576 | tf_op jit(solution)/shard_map/all_to_all | solution.py:119
  10.5 0.2 copy.29
  10.9 0.8 pad_maximum_fusion
  11.7 13.3 %all-to-all-done.1 = bf16[128,8,256]{0,2,1:T(8,128)(2,1)S(1)} async-done(((bf16[128,8,256]{0,2,1:T(8,128)(2,1)}), bf16[128,8,256]{0,2,1:T(8,128)(2,1)S(1)}, u32[]{:S(2)}, u32[]{:S(2)}) %all-to-all-start.1) | async-done | bytes 524320 | tf_op jit(solution)/shard_map/all_to_all | solution.py:119
  25.0 3.6 %all-to-all-start = ((bf16[128,8,256]{0,2,1:T(8,128)(2,1)}), bf16[128,8,256]{0,2,1:T(8,128)(2,1)S(1)}, u32[]{:S(2)}, u32[]{:S(2)}) async-start(bf16[128,8,256]{0,2,1:T(8,128)(2,1)} %bitcast.4), calls=%async_computation | async-start | bytes 1048576 | tf_op jit(solution)/shard_map/all_to_all | solution.py:118
  28.6 1.0 copy.33
  29.7 13.6 %all-to-all-done = bf16[128,8,256]{0,2,1:T(8,128)(2,1)S(1)} async-done(((bf16[128,8,256]{0,2,1:T(8,128)(2,1)}), bf16[128,8,256]{0,2,1:T(8,128)(2,1)S(1)}, u32[]{:S(2)}, u32[]{:S(2)}) %all-to-all-start) | async-done | bytes 524320 | tf_op jit(solution)/shard_map/all_to_all | solution.py:118
  43.3 3.6 %all-to-all-start.2 = ((bf16[128,8,256]{0,2,1:T(8,128)(2,1)}), bf16[128,8,256]{0,2,1:T(8,128)(2,1)S(1)}, u32[]{:S(2)}, u32[]{:S(2)}) async-start(bf16[128,8,256]{0,2,1:T(8,128)(2,1)} %bitcast.11), calls=%async_computation.2 | async-start | bytes 1048576 | tf_op jit(solution)/shard_map/all_to_all | solution.py:120
  47.0 0.3 copy.32
  47.3 0.2 reshape.294
  47.5 0.3 copy.36
  47.8 0.2 copy.30
  48.2 13.5 %all-to-all-done.2 = bf16[128,8,256]{0,2,1:T(8,128)(2,1)S(1)} async-done(((bf16[128,8,256]{0,2,1:T(8,128)(2,1)}), bf16[128,8,256]{0,2,1:T(8,128)(2,1)S(1)}, u32[]{:S(2)}, u32[]{:S(2)}) %all-to-all-start.2) | async-done | bytes 524320 | tf_op jit(solution)/shard_map/all_to_all | solution.py:120
  61.6 0.3 copy.34
  62.0 0.2 reshape.295
  62.2 0.3 copy.37
  62.5 15.3 %while.10 = (s32[]{:T(128)}, bf16[2,512,2,128]{3,2,1,0:T(2,128)(2,1)}, bf16[2,512,2,128]{3,2,1,0:T(2,128)(2,1)S(1)}, bf16[1024,2,128]{2,0,1:T(8,128)(2,1)S(1)}, bf16[1024,2,128]{2,0,1:T(8,128)(2,1)S(1)}, /*index=5*/s32[]{:T(128)}) while((s32[]{:T(128)}, bf16[2,512,2,128]{3,2,1,0:T(2,128)(2,1)}, bf16[2,512,2,128]{3,2,1,0:T(2,128)(2,1)S(1)}, ...), condition=%wide.region_3.4_spmd, body=%wide.region_0.3_spmd.sunk | while | flops 542245888 | bytes 15212677 | solution.py:66
  62.7 3.4 %fusion.110 = (f32[2,512]{1,0:T(2,128)S(1)}, f32[2,512,1024]{2,1,0:T(8,128)}) fusion(bf16[1024,2,128]{2,0,1:T(8,128)(2,1)S(1)} %get-tuple-element.153, bf16[1,512,2,128]{3,2,1,0:T(2,128)(2,1)S(1)} %constant_dynamic-slice_fusion.2), kind=kOutput, calls=%fused_computation.160.clone.1 | convolution fusion | flops 271582208 | bytes 4984832 | tf_op jit(solution)/shard_map/while/body/eval_jaxpr/sub | solution.py:60
  66.0 3.0 %fusion.111 = bf16[1,512,2,128]{3,1,2,0:T(8,128)(2,1)S(1)} fusion(bf16[1024,2,128]{2,0,1:T(8,128)(2,1)S(1)} %get-tuple-element.154, f32[2,512,1024]{2,1,0:T(8,128)} %get-tuple-element.136, f32[2,512]{1,0:T(2,128)S(1)} %get-tuple-element.137), kind=kOutput, calls=%fused_computation.8.clone.1 | convolution fusion | flops 270663680 | bytes 4984832 | tf_op jit(solution)/shard_map/while/body/eval_jaxpr/hqk,khd->qhd/dot_general | solution.py:62
  69.1 0.3 copy_dynamic-update-slice_fusion.2
  69.4 0.8 copy-done.12
  70.3 3.4 %fusion.110 = (f32[2,512]{1,0:T(2,128)S(1)}, f32[2,512,1024]{2,1,0:T(8,128)}) fusion(bf16[1024,2,128]{2,0,1:T(8,128)(2,1)S(1)} %get-tuple-element.153, bf16[1,512,2,128]{3,2,1,0:T(2,128)(2,1)S(1)} %constant_dynamic-slice_fusion.2), kind=kOutput, calls=%fused_computation.160.clone.1 | convolution fusion | flops 271582208 | bytes 4984832 | tf_op jit(solution)/shard_map/while/body/eval_jaxpr/sub | solution.py:60
  73.7 3.0 %fusion.111 = bf16[1,512,2,128]{3,1,2,0:T(8,128)(2,1)S(1)} fusion(bf16[1024,2,128]{2,0,1:T(8,128)(2,1)S(1)} %get-tuple-element.154, f32[2,512,1024]{2,1,0:T(8,128)} %get-tuple-element.136, f32[2,512]{1,0:T(2,128)S(1)} %get-tuple-element.137), kind=kOutput, calls=%fused_computation.8.clone.1 | convolution fusion | flops 270663680 | bytes 4984832 | tf_op jit(solution)/shard_map/while/body/eval_jaxpr/hqk,khd->qhd/dot_general | solution.py:62
  76.7 0.3 copy_dynamic-update-slice_fusion.2
  77.0 0.8 copy-done.12
  77.8 2.2 %reshape_reshape.7 = bf16[8,128,256]{2,1,0:T(8,128)(2,1)} reshape(bf16[2,512,2,128]{3,2,1,0:T(2,128)(2,1)} %get-tuple-element.30) | data formatting | bytes 1048576 | tf_op jit(solution)/shard_map/reshape;reshape | solution.py:167
  80.0 3.6 %all-to-all-start.3 = ((bf16[8,128,256]{2,1,0:T(8,128)(2,1)}), bf16[8,128,256]{2,1,0:T(8,128)(2,1)S(1)}, u32[]{:S(2)}, u32[]{:S(2)}) async-start(bf16[8,128,256]{2,1,0:T(8,128)(2,1)} %reshape_reshape.7), calls=%async_computation.3 | async-start | bytes 1048576 | tf_op jit(solution)/shard_map/all_to_all | solution.py:168
  83.6 14.7 %all-to-all-done.3 = bf16[8,128,256]{2,1,0:T(8,128)(2,1)S(1)} async-done(((bf16[8,128,256]{2,1,0:T(8,128)(2,1)}), bf16[8,128,256]{2,1,0:T(8,128)(2,1)S(1)}, u32[]{:S(2)}, u32[]{:S(2)}) %all-to-all-start.3) | async-done | bytes 524320 | tf_op jit(solution)/shard_map/all_to_all | solution.py:168
  98.3 0.3 copy.39
  98.6 0.4 fusion.80
  99.2 0.4 fusion.26
  99.6 3.4 %collective-permute-start = (bf16[2,64,256]{2,1,0:T(8,128)(2,1)S(1)}, bf16[2,64,256]{2,1,0:T(8,128)(2,1)S(1)}, u32[]{:S(2)}, u32[]{:S(2)}) collective-permute-start(bf16[2,64,256]{2,1,0:T(8,128)(2,1)S(1)} %bitcast.184), channel_id=1, source_target_pairs={{0,1},{1,2},{2,3},{3,4},{4,5},{5,6},{6,7},{8,9},{9,10},{10,11},{11... | collective-permute-start | bytes 196616 | tf_op jit(solution)/shard_map/ppermute | solution.py:22
  103.0 1.5 collective-permute-start.1
  104.5 0.4 collective-permute-done
  104.9 4.3 %collective-permute-done.1 = bf16[2,64,256]{2,1,0:T(8,128)(2,1)S(1)} collective-permute-done((bf16[2,64,256]{2,1,0:T(8,128)(2,1)S(1)}, bf16[2,64,256]{2,1,0:T(8,128)(2,1)S(1)}, u32[]{:S(2)}, u32[]{:S(2)}) %collective-permute-start.1) | collective-permute-done | bytes 65568 | tf_op jit(solution)/shard_map/ppermute | solution.py:25
  111.2 0.6 fusion.16
  111.9 0.4 broadcast_in_dim.54
  112.4 1.2 reshape.310
  113.7 6.8 %pad_slice_fusion = (bf16[8,256,256]{2,1,0:T(8,128)(2,1)}, bf16[8,256,256]{2,1,0:T(8,128)(2,1)}, bf16[8,256,256]{2,1,0:T(8,128)(2,1)}, bf16[8,256,256]{2,1,0:T(8...) fusion(bf16[10,256,256]{2,1,0:T(8,128)(2,1)} %reshape.310), kind=kLoop, calls=%fused_computation.31 | loop fusion | bytes 7602176 | tf_op jit(solution)/shard_map/slice | solution.py:94
  120.5 0.3 broadcast_in_dim.55
  120.8 1.1 reshape.312
  122.0 0.3 broadcast_in_dim.57
  122.2 0.3 reshape.315
  122.5 1.4 broadcast_in_dim.58
  123.9 1.4 reshape.318
  125.3 1.7 %fusion.63 = f32[2048,16]{0,1:T(8,128)S(1)} fusion(bf16[2048,256]{1,0:T(8,128)(2,1)} %bitcast.173, bf16[9,16,256]{2,1,0:T(8,128)(2,1)S(1)} %copy-done.13), kind=kOutput, calls=%fused_computation.135 | convolution fusion | flops 16777216 | bytes 1187840 | tf_op jit(solution)/shard_map/dot_general | solution.py:97
  127.1 0.4 convolution_add_fusion.7
  127.5 0.4 convolution_add_fusion.6
  127.8 0.5 copy-done.4
  128.3 0.4 convolution_add_fusion.5
  128.7 0.4 convolution_add_fusion.4
  129.1 0.5 copy-done.3
  129.5 0.4 convolution_add_fusion.3
  130.0 0.4 convolution_add_fusion.2
  130.4 0.4 convolution_add_fusion.1
  130.8 0.5 copy-done.6
  131.2 0.4 fusion.54
  131.8 0.6 fusion.77
  132.4 0.6 sub.68
  133.0 19.4 %psum.7 = f32[]{:T(128)} all-reduce(f32[]{:T(128)} %get-tuple-element.58), channel_id=1, replica_groups=mesh['crop'=4,'seq'=8] {'seq'}, use_global_device_ids=true, to_apply=%region_10.11 | all-reduce | flops 1 | bytes 8 | tf_op jit(solution)/shard_map/psum | solution.py:194
  152.4 0.7 bitcast_add_fusion
  (68 shorter events, 3.5 us)
Async XLA Ops:
  0.6 97.9 %copy-start = (bf16[2048,256]{1,0:T(8,128)(2,1)S(1)}, bf16[2048,256]{1,0:T(8,128)(2,1)}, u32[]{:S(2)}) copy-start(bf16[2048,256]{1,0:T(8,128)(2,1)} %param.15) | copy-start | bytes 3145732
  2.4 8.2 %copy-start.9 = (bf16[128,2048]{1,0:T(8,128)(2,1)S(1)}, bf16[128,2048]{1,0:T(8,128)(2,1)}, u32[]{:S(2)}) copy-start(bf16[128,2048]{1,0:T(8,128)(2,1)} %param.12) | copy-start | bytes 1572868
  3.2 21.8 %all-to-all-start.1 = ((bf16[128,8,256]{0,2,1:T(8,128)(2,1)}), bf16[128,8,256]{0,2,1:T(8,128)(2,1)S(1)}, u32[]{:S(2)}, u32[]{:S(2)}) async-start(bf16[128,8,256]{0,2,1:T(8,128)(2,1)} %bitcast.8), calls=%async_computation.1 | async-start | bytes 1048576 | tf_op jit(solution)/shard_map/all_to_all | solution.py:119
  10.9 17.8 %copy-start.10 = (bf16[128,2048]{1,0:T(8,128)(2,1)S(1)}, bf16[128,2048]{1,0:T(8,128)(2,1)}, u32[]{:S(2)}) copy-start(bf16[128,2048]{1,0:T(8,128)(2,1)} %param.14) | copy-start | bytes 1572868
  25.0 18.3 %all-to-all-start = ((bf16[128,8,256]{0,2,1:T(8,128)(2,1)}), bf16[128,8,256]{0,2,1:T(8,128)(2,1)S(1)}, u32[]{:S(2)}, u32[]{:S(2)}) async-start(bf16[128,8,256]{0,2,1:T(8,128)(2,1)} %bitcast.4), calls=%async_computation | async-start | bytes 1048576 | tf_op jit(solution)/shard_map/all_to_all | solution.py:118
  43.3 18.3 %all-to-all-start.2 = ((bf16[128,8,256]{0,2,1:T(8,128)(2,1)}), bf16[128,8,256]{0,2,1:T(8,128)(2,1)S(1)}, u32[]{:S(2)}, u32[]{:S(2)}) async-start(bf16[128,8,256]{0,2,1:T(8,128)(2,1)} %bitcast.11), calls=%async_computation.2 | async-start | bytes 1048576 | tf_op jit(solution)/shard_map/all_to_all | solution.py:120
  66.0 3.0 %copy-start.11 = (bf16[2,512,2,128]{3,2,1,0:T(2,128)(2,1)S(1)}, bf16[2,512,2,128]{3,2,1,0:T(2,128)(2,1)}, u32[]{:S(2)}) copy-start(bf16[2,512,2,128]{3,2,1,0:T(2,128)(2,1)} %get-tuple-element.145) | copy-start | bytes 1572868 | tf_op jit(solution)/shard_map/while
  69.4 0.8 copy-start.12
  73.7 3.0 %copy-start.11 = (bf16[2,512,2,128]{3,2,1,0:T(2,128)(2,1)S(1)}, bf16[2,512,2,128]{3,2,1,0:T(2,128)(2,1)}, u32[]{:S(2)}) copy-start(bf16[2,512,2,128]{3,2,1,0:T(2,128)(2,1)} %get-tuple-element.145) | copy-start | bytes 1572868 | tf_op jit(solution)/shard_map/while
  77.0 0.8 copy-start.12
  77.8 5.8 %copy-start.14 = (s32[8,256]{1,0:T(8,128)S(1)}, s32[8,256]{1,0:T(8,128)}, u32[]{:S(2)}) copy-start(s32[8,256]{1,0:T(8,128)} %param.21) | copy-start | bytes 24580
  80.0 18.3 %all-to-all-start.3 = ((bf16[8,128,256]{2,1,0:T(8,128)(2,1)}), bf16[8,128,256]{2,1,0:T(8,128)(2,1)S(1)}, u32[]{:S(2)}, u32[]{:S(2)}) async-start(bf16[8,128,256]{2,1,0:T(8,128)(2,1)} %reshape_reshape.7), calls=%async_computation.3 | async-start | bytes 1048576 | tf_op jit(solution)/shard_map/all_to_all | solution.py:168
  98.3 0.9 copy-start.16
  99.0 10.3 %copy-start.7 = (bf16[9,256,256]{2,1,0:T(8,128)(2,1)S(1)}, bf16[9,256,256]{2,1,0:T(8,128)(2,1)}, u32[]{:S(2)}) copy-start(bf16[9,256,256]{2,1,0:T(8,128)(2,1)} %param.17) | copy-start | bytes 3538948
  99.6 5.3 %collective-permute-start = (bf16[2,64,256]{2,1,0:T(8,128)(2,1)S(1)}, bf16[2,64,256]{2,1,0:T(8,128)(2,1)S(1)}, u32[]{:S(2)}, u32[]{:S(2)}) collective-permute-start(bf16[2,64,256]{2,1,0:T(8,128)(2,1)S(1)} %bitcast.184), channel_id=1, source_target_pairs={{0,1},{1,2},{2,3},{3,4},{4,5},{5,6},{6,7},{8,9},{9,10},{10,11},{11... | collective-permute-start | bytes 196616 | tf_op jit(solution)/shard_map/ppermute | solution.py:22
  103.0 6.2 %collective-permute-start.1 = (bf16[2,64,256]{2,1,0:T(8,128)(2,1)S(1)}, bf16[2,64,256]{2,1,0:T(8,128)(2,1)S(1)}, u32[]{:S(2)}, u32[]{:S(2)}) collective-permute-start(bf16[2,64,256]{2,1,0:T(8,128)(2,1)S(1)} %bitcast.185), channel_id=1, source_target_pairs={{1,0},{2,1},{3,2},{4,3},{5,4},{6,5},{7,6},{9,8},{10,9},{11,10},{12... | collective-permute-start | bytes 196616 | tf_op jit(solution)/shard_map/ppermute | solution.py:25
  110.5 0.7 copy-start.17
  111.8 0.7 copy-start.8
  120.8 1.2 slice-start
  123.9 1.4 copy-start.13
  125.3 1.8 %copy-start.1 = (bf16[2048,256]{1,0:T(8,128)(2,1)S(1)}, bf16[2048,256]{1,0:T(8,128)(2,1)}, u32[]{:S(2)}) copy-start(bf16[2048,256]{1,0:T(8,128)(2,1)} %reshape.312) | copy-start | bytes 3145732
  125.3 2.2 %copy-start.5 = (bf16[8,256,256]{2,1,0:T(8,128)(2,1)S(1)}, bf16[8,256,256]{2,1,0:T(8,128)(2,1)}, u32[]{:S(2)}) copy-start(bf16[8,256,256]{2,1,0:T(8,128)(2,1)} %get-tuple-element.63) | copy-start | bytes 3145732
  127.1 1.3 copy-start.4
  128.3 1.2 copy-start.3
  128.7 1.3 copy-start.2
  130.0 1.2 copy-start.6
  130.0 1.2 copy-start.15
where the time goes:
time: 156 us; the launch traced here: 155 us
  waiting for transfers between devices  59.7 us (38%)
  local copies, waits for them, and re-layouts  25.4 us (16%)
  starting transfers between devices  23 us (15%)
  matrix products  19.6 us (13%)
  blocking collectives  19.4 us (12%)
  other arithmetic  4.92 us (3%)
  between operations  2.86 us (2%)
    psum x1, blocking collectives, body(): summed_loss = lax.psum(jnp.sum(losses), 'seq')  19.4 us
    all_to_all x1, waiting for transfers between devices, body(): lax.all_to_all(outgoing, 'seq', split_axis=0, concat_axis=0, tiled=True)  14.7 us
    all_to_all x1, waiting for transfers between devices, to_heads(): lax.all_to_all(query_send, 'seq', split_axis=1, concat_axis=0, tiled=True)  13.6 us
    all_to_all x1, waiting for transfers between devices, to_heads(): lax.all_to_all(value_send, 'seq', split_axis=1, concat_axis=0, tiled=True)  13.5 us
    all_to_all x1, waiting for transfers between devices, to_heads(): lax.all_to_all(key_send, 'seq', split_axis=1, concat_axis=0, tiled=True)  13.3 us
    all_to_all x1, starting transfers between devices, to_heads(): lax.all_to_all(key_send, 'seq', split_axis=1, concat_axis=0, tiled=True)  7.28 us
    slice x4, local copies, waits for them, and re-layouts, classify(): padded[tap_row:tap_row + out_rows, tap_col:tap_col + out_cols]  6.88 us
    sub x2, matrix products, one_block(): exponent = jnp.exp(scores - highest)  6.71 us
  transfers between devices with their start and end apart: 6, of which 6 were waited for; matrix products, arithmetic and copies ran while one was open for 2% of the time, Pallas kernels for 0%

commit v1 on v0

v1 whole, which is shorter than its diff:
```python
import functools
import math

import jax
import jax.numpy as jnp
import numpy as np
from jax import lax
from jax.experimental import pallas as pl
from jax.experimental.pallas import tpu as pltpu
from jax.sharding import PartitionSpec as P

HEADS = 16
HEAD_DIM = 128
UPSCALE = 4
GRID_COLS = 64
EPSILON = 1e-05
MESH = pl.DeviceIdType.MESH
F32 = jnp.float32
BF16 = jnp.bfloat16


def gelu(x):
    return 0.5 * x * (1.0 + lax.erf(x * (2.0**-0.5)))


def tables(grid_rows):
    quarter = HEAD_DIM // 4
    omegas = np.power(np.float32(100.0), -np.arange(quarter, dtype=np.float32) / quarter)

    def half(count, offset):
        angles = np.arange(count, dtype=np.float32)[:, None] * omegas[None, :].astype(np.float32)
        cosine = np.cos(angles.astype(np.float64)).astype(np.float32)
        sine = np.sin(angles.astype(np.float64)).astype(np.float32)
        out = np.zeros((3, count, HEAD_DIM), np.float32)
        out[0, :, offset : offset + quarter] = cosine
        out[0, :, offset + quarter : offset + 2 * quarter] = cosine
        out[1, :, offset : offset + quarter] = -sine
        out[2, :, offset + quarter : offset + 2 * quarter] = sine
        return out

    return half(grid_rows, 0), half(GRID_COLS, 2 * quarter)


def kernel(
    n,
    q_ref,
    k_ref,
    v_ref,
    pw_ref,
    gain_ref,
    cw_ref,
    cb_ref,
    tw_ref,
    tb_ref,
    lab_ref,
    row_ref,
    col_ref,
    up_ref,
    logits_ref,
    losses_ref,
    loss_ref,
    qx,
    kx,
    pw,
    cw,
    rq,
    rk,
    qbuf,
    kbuf,
    vbuf,
    obuf,
    mix,
    ext,
    part_sum,
    sums,
    ssem,
    rsem,
    osend,
    orecv,
    hsend,
    hrecv,
    lsend,
    lrecv,
    local,
):
    me = lax.axis_index("seq")
    hpd, keys, dim = kbuf.shape
    tokens = keys // n
    part = qbuf.shape[1] // n
    split = tokens // part
    strip = tokens // GRID_COLS
    my_group = me // split
    my_part = lax.rem(me, split)

    def peer(i):
        off = n // 2 + ((i + 1) // 2) * (1 - 2 * lax.rem(i, 2))
        return lax.rem(me + off, n)

    def each_peer(fn):
        def step(i, carry):
            fn(peer(i))
            return carry

        lax.fori_loop(0, n - 1, step, 0)

    barrier = pltpu.get_barrier_semaphore()
    each_peer(
        lambda d: pl.semaphore_signal(barrier, inc=1, device_id={"seq": d}, device_id_type=MESH)
    )
    load_k = pltpu.make_async_copy(k_ref, kx, local.at[0])
    load_q = pltpu.make_async_copy(q_ref, qx, local.at[1])
    load_pw = pltpu.make_async_copy(pw_ref, pw, local.at[2])
    load_cw = pltpu.make_async_copy(cw_ref, cw, local.at[3])
    load_k.start()
    load_q.start()
    own_v = []
    for h in range(hpd):
        cols = pl.ds(pl.multiple_of((my_group * hpd + h) * dim, dim), dim)
        rows = pl.ds(pl.multiple_of(me * tokens, tokens), tokens)
        copy = pltpu.make_async_copy(v_ref.at[:, cols], vbuf.at[h, rows], local.at[4 + h])
        copy.start()
        own_v.append(copy)
    load_pw.start()
    load_cw.start()

    turn = []
    for t in range(3):
        pieces = []
        for r in range(strip):
            pieces.append(row_ref[t, pl.ds(me * strip + r, 1), :] + col_ref[t])
        turn.append(jnp.concatenate(pieces, axis=0) if strip > 1 else pieces[0])

    def rotate(src, dst, h):
        for g in range(HEADS // hpd):
            head = g * hpd + h
            x = src[:, head * dim : (head + 1) * dim].astype(F32)
            out = x * turn[0] + pltpu.roll(x, 96, 1) * turn[1] + pltpu.roll(x, 32, 1) * turn[2]
            dst[head] = out.astype(BF16)

    def v_copy(h, d, s):
        head = (d // split) * hpd + h
        return pltpu.make_async_remote_copy(
            src_ref=v_ref.at[:, pl.ds(pl.multiple_of(head * dim, dim), dim)],
            dst_ref=vbuf.at[h, pl.ds(pl.multiple_of(s * tokens, tokens), tokens)],
            send_sem=ssem.at[0, h, d],
            recv_sem=rsem.at[0, h, s],
            device_id={"seq": d},
            device_id_type=MESH,
        )

    def k_copy(h, d, s):
        return pltpu.make_async_remote_copy(
            src_ref=rk.at[(d // split) * hpd + h],
            dst_ref=kbuf.at[h, pl.ds(pl.multiple_of(s * tokens, tokens), tokens)],
            send_sem=ssem.at[1, h, d],
            recv_sem=rsem.at[1, h, s],
            device_id={"seq": d},
            device_id_type=MESH,
        )

    def q_copy(h, d, s):
        rows = pl.ds(pl.multiple_of(lax.rem(d, split) * part, part), part)
        return pltpu.make_async_remote_copy(
            src_ref=rq.at[(d // split) * hpd + h, rows],
            dst_ref=qbuf.at[h, pl.ds(pl.multiple_of(s * part, part), part)],
            send_sem=ssem.at[2, h, d],
            recv_sem=rsem.at[2, h, s],
            device_id={"seq": d},
            device_id_type=MESH,
        )

    load_k.wait()
    rotate(kx, rk, 0)
    pl.semaphore_wait(barrier, n - 1)
    for h in range(hpd):
        if h > 0:
            rotate(kx, rk, h)
        each_peer(lambda d: k_copy(h, d, me).start())
        if h == 0:
            load_q.wait()
        rotate(qx, rq, h)
        each_peer(lambda d: q_copy(h, d, me).start())
        each_peer(lambda d: v_copy(h, d, me).start())
        head = my_group * hpd + h
        kbuf[h, pl.ds(pl.multiple_of(me * tokens, tokens), tokens), :] = rk[head]
        qbuf[h, pl.ds(pl.multiple_of(me * part, part), part), :] = rq[
            head, pl.ds(pl.multiple_of(my_part * part, part), part), :
        ]

    def o_copy(h, d, s):
        head = (s // split) * hpd + h
        return pltpu.make_async_remote_copy(
            src_ref=obuf.at[h, pl.ds(pl.multiple_of(d * part, part), part)],
            dst_ref=mix.at[
                pl.ds(pl.multiple_of(lax.rem(s, split) * part, part), part),
                pl.ds(pl.multiple_of(head * dim, dim), dim),
            ],
            send_sem=osend.at[h, d],
            recv_sem=orecv.at[h, s],
            device_id={"seq": d},
            device_id_type=MESH,
        )

    block = min(256, n * part)
    in_block = block // part
    blocks = n * part // block
    factor = dim ** (-0.5) * math.log2(math.e)

    for h in range(hpd):
        each_peer(lambda s: k_copy(h, s, s).wait_recv())
        each_peer(lambda s: q_copy(h, s, s).wait_recv())
        own_v[h].wait()
        each_peer(lambda s: v_copy(h, s, s).wait_recv())

        def attend(i, carry):
            j = lax.rem(me // in_block + blocks // 2 + i, blocks)
            rows = pl.ds(pl.multiple_of(j * block, block), block)
            scores = lax.dot_general(
                qbuf[h, rows, :], kbuf[h], (((1,), (1,)), ((), ())), preferred_element_type=F32
            )
            highest = jnp.max(scores, axis=1, keepdims=True)
            exponent = jnp.exp2((scores - highest) * factor)
            total = jnp.sum(exponent, axis=1, keepdims=True)
            weights = (exponent * (1.0 / total)).astype(BF16)
            mixed = jnp.dot(weights, vbuf[h], preferred_element_type=F32)
            obuf[h, rows, :] = mixed.astype(BF16)
            for u in range(in_block):
                d = j * in_block + u

                @pl.when(d != me)
                def _():
                    o_copy(h, d, me).start()

            return carry

        lax.fori_loop(0, blocks, attend, 0, unroll=blocks <= 4)
        head = my_group * hpd + h
        mix[
            pl.ds(pl.multiple_of(my_part * part, part), part),
            pl.ds(pl.multiple_of(head * dim, dim), dim),
        ] = obuf[h, pl.ds(pl.multiple_of(me * part, part), part), :]

    load_pw.wait()
    for h in range(hpd):
        each_peer(lambda s: o_copy(h, s, s).wait_recv())
    features = jnp.dot(mix[...], pw[...], preferred_element_type=F32)
    center = jnp.mean(features, axis=-1, keepdims=True)
    shifted = features - center
    spread = jnp.mean(shifted * shifted, axis=-1, keepdims=True)
    act = gelu(shifted / jnp.sqrt(spread + EPSILON) * gain_ref[...]).astype(BF16)
    cols = GRID_COLS
    halo = 2 * cols
    ext[halo : halo + tokens, :] = act

    up, down = lax.rem(me + 1, n), lax.rem(me + n - 1, n)
    to_up = pltpu.make_async_remote_copy(
        src_ref=ext.at[tokens : tokens + halo],
        dst_ref=ext.at[0:halo],
        send_sem=hsend.at[0],
        recv_sem=hrecv.at[0],
        device_id={"seq": up},
        device_id_type=MESH,
    )
    to_down = pltpu.make_async_remote_copy(
        src_ref=ext.at[halo : 2 * halo],
        dst_ref=ext.at[halo + tokens : 2 * halo + tokens],
        send_sem=hsend.at[1],
        recv_sem=hrecv.at[1],
        device_id={"seq": down},
        device_id_type=MESH,
    )
    to_up.start()
    to_down.start()
    load_cw.wait()
    to_up.wait()
    to_down.wait()

    place = lax.broadcasted_iota(jnp.int32, (tokens + 2 * halo, 1), 0)
    grid_row = place // cols + (me * strip - 2)
    inside = (grid_row >= 0) & (grid_row < strip * n)
    window = jnp.where(inside, ext[...].astype(F32), 0.0).astype(BF16)
    count = tokens + 2 * cols
    by_col = []
    for s in range(3):
        summed = None
        for r in range(3):
            term = jnp.dot(
                window[r * cols : r * cols + count], cw[3 * r + s], preferred_element_type=F32
            )
            summed = term if summed is None else summed + term
        by_col.append(summed)
    column = lax.rem(lax.broadcasted_iota(jnp.int32, (count, 1), 0), cols)
    conv = (
        by_col[1]
        + jnp.where(column == 0, 0.0, pltpu.roll(by_col[0], 1, 0))
        + jnp.where(column == cols - 1, 0.0, pltpu.roll(by_col[2], count - 1, 0))
    )
    hidden = jnp.where(inside[cols : cols + count], gelu(conv + cb_ref[...]), 0.0).astype(BF16)

    width = cols * UPSCALE
    lane = lax.broadcasted_iota(jnp.int32, (1, width), 1)
    classes = tb_ref.shape[0]
    rows_of = []
    for r in range(strip + 2):
        wide = jnp.dot(
            up_ref[...], hidden[r * cols : (r + 1) * cols], preferred_element_type=F32
        ).astype(BF16)
        taps = lax.dot_general(
            tw_ref[...], wide, (((1,), (1,)), ((), ())), preferred_element_type=F32
        )
        tap = lambda i: taps[i * classes : (i + 1) * classes]
        rows_of.append(
            [
                tap(3 * t + 1)
                + jnp.where(lane == 0, 0.0, pltpu.roll(tap(3 * t), 1, 1))
                + jnp.where(lane == width - 1, 0.0, pltpu.roll(tap(3 * t + 2), width - 1, 1))
                for t in range(3)
            ]
        )
    bias = tb_ref[...]
    ids = lax.broadcasted_iota(jnp.int32, (classes, width), 0)
    running = jnp.zeros((1, width), F32)
    for r in range(strip):
        low, here, high = rows_of[r], rows_of[r + 1], rows_of[r + 2]
        inner = here[0] + here[1] + here[2] + bias
        for phase in range(UPSCALE):
            if phase == 0:
                out = low[0] + here[1] + here[2] + bias
            elif phase == UPSCALE - 1:
                out = here[0] + here[1] + high[2] + bias
            else:
                out = inner
            y = r * UPSCALE + phase
            logits_ref[:, y, :] = out
            if phase != 2:
                highest = jnp.max(out, axis=0, keepdims=True)
                lse = highest + jnp.log(jnp.sum(jnp.exp(out - highest), axis=0, keepdims=True))
            picked = jnp.sum(
                jnp.where(ids == lab_ref[y : y + 1, :], out, 0.0), axis=0, keepdims=True
            )
            lost = lse - picked
            losses_ref[y : y + 1, :] = lost
            running = running + lost

    total = jnp.sum(running, axis=1, keepdims=True)
    part_sum[...] = jnp.broadcast_to(total, part_sum.shape)

    def l_copy(d, s):
        return pltpu.make_async_remote_copy(
            src_ref=part_sum,
            dst_ref=sums.at[s],
            send_sem=lsend.at[d],
            recv_sem=lrecv.at[s],
            device_id={"seq": d},
            device_id_type=MESH,
        )

    each_peer(lambda d: l_copy(d, me).start())
    sums[me] = part_sum[...]
    for h in range(hpd):
        each_peer(lambda d: v_copy(h, d, me).wait_send())
        each_peer(lambda d: k_copy(h, d, me).wait_send())
        each_peer(lambda d: q_copy(h, d, me).wait_send())
        each_peer(lambda d: o_copy(h, d, me).wait_send())
    each_peer(lambda s: l_copy(s, s).wait_recv())
    each_peer(lambda d: l_copy(d, me).wait_send())
    pixels = n * strip * UPSCALE * width
    loss_ref[...] = jnp.sum(sums[...], axis=0)[0:1, 0:1] / pixels


def body(
    queries,
    keys,
    values,
    proj_weight,
    norm_gain,
    conv_weight,
    conv_bias,
    class_weight,
    class_bias,
    labels,
):
    n = lax.axis_size("seq")
    tokens = queries.shape[0]
    strip = tokens // GRID_COLS
    hpd = max(1, HEADS // n)
    split = max(1, n // HEADS)
    part = tokens // split
    channels = proj_weight.shape[1]
    classes = class_weight.shape[1]
    row_table, col_table = tables(strip * n)
    spread = np.zeros((GRID_COLS * UPSCALE, GRID_COLS), np.float32)
    spread[np.arange(GRID_COLS * UPSCALE), np.arange(GRID_COLS * UPSCALE) // UPSCALE] = 1.0
    hbm = pl.BlockSpec(memory_space=pl.ANY)
    vmem = pl.BlockSpec(memory_space=pltpu.VMEM)
    dma = pltpu.SemaphoreType.DMA
    logits, losses, loss = pl.pallas_call(
        functools.partial(kernel, n),
        out_shape=(
            jax.ShapeDtypeStruct((classes,) + labels.shape, F32),
            jax.ShapeDtypeStruct(labels.shape, F32),
            jax.ShapeDtypeStruct((1, 1), F32),
        ),
        in_specs=[hbm, hbm, hbm, hbm, vmem, hbm] + [vmem] * 7,
        out_specs=(vmem, vmem, vmem),
        scratch_shapes=[
            pltpu.VMEM((tokens, HEADS * HEAD_DIM), BF16),
            pltpu.VMEM((tokens, HEADS * HEAD_DIM), BF16),
            pltpu.VMEM(proj_weight.shape, BF16),
            pltpu.VMEM(conv_weight.shape, BF16),
            pltpu.VMEM((HEADS, tokens, HEAD_DIM), BF16),
            pltpu.VMEM((HEADS, tokens, HEAD_DIM), BF16),
            pltpu.VMEM((hpd, n * part, HEAD_DIM), BF16),
            pltpu.VMEM((hpd, n * tokens, HEAD_DIM), BF16),
            pltpu.VMEM((hpd, n * tokens, HEAD_DIM), BF16),
            pltpu.VMEM((hpd, n * part, HEAD_DIM), BF16),
            pltpu.VMEM((tokens, HEADS * HEAD_DIM), BF16),
            pltpu.VMEM((tokens + 4 * GRID_COLS, channels), BF16),
            pltpu.VMEM((8, 128), F32),
            pltpu.VMEM((n, 8, 128), F32),
            dma((3, hpd, n)),
            dma((3, hpd, n)),
            dma((hpd, n)),
            dma((hpd, n)),
            dma((2,)),
            dma((2,)),
            dma((n,)),
            dma((n,)),
            dma((4 + hpd,)),
        ],
        compiler_params=pltpu.CompilerParams(
            collective_id=0, has_side_effects=True, vmem_limit_bytes=56 * 1024 * 1024
        ),
    )(
        queries,
        keys,
        values,
        proj_weight,
        norm_gain.reshape(1, -1),
        conv_weight,
        conv_bias.reshape(1, -1),
        class_weight.reshape(-1, class_weight.shape[2]),
        class_bias.reshape(-1, 1),
        labels,
        jnp.asarray(row_table),
        jnp.asarray(col_table),
        jnp.asarray(spread, BF16),
    )
    return logits, losses, loss.reshape(1)


def solution(mesh):
    rows = P(("crop", "seq"), None)
    in_specs = (rows, rows, rows, P(), P(), P(), P(), P(), P(), rows)
    out_specs = (P(None, ("crop", "seq"), None), rows, P("crop"))
    return jax.shard_map(body, mesh=mesh, in_specs=in_specs, out_specs=out_specs, check_vma=False)
```

time: 156 us -> 72.6 us (0.47)
  Pallas kernels: 0 us -> 65.7 us
  waiting for transfers between devices: 59.7 us -> 0 us
  starting transfers between devices: 23 us -> 0 us
  local copies, waits for them, and re-layouts: 25.4 us -> 4.19 us
  matrix products: 19.6 us -> 0 us
  blocking collectives: 19.4 us -> 0 us
  other arithmetic: 4.92 us -> 0 us
    pallas_call x0 -> x1, Pallas kernels: none -> 65.7 us  [body(): pl.pallas_call(functools.partial(kernel, n), out_shape=(jax.ShapeDtypeStr...]
    all_to_all x4 -> x0, waiting for transfers between devices: 55 us -> none  [the longest x1 14.7 us: body(): lax.all_to_all(outgoing, 'seq', split_axis=0, concat_axis=0, tiled=True)]
    psum x1 -> x0, blocking collectives: 19.4 us -> none  [body(): summed_loss = lax.psum(jnp.sum(losses), 'seq')]
    all_to_all x4 -> x0, starting transfers between devices: 18.2 us -> none  [the longest x1 7.28 us: to_heads(): lax.all_to_all(key_send, 'seq', split_axis=1, concat_axis=0, tiled=True)]
    dot_general x21 -> x0, matrix products: 12.9 us -> none  [the longest x2 6 us: one_block(): jnp.einsum('hqk,khd->qhd', weights, values, preferred_element_type=jnp.fl...]
    slice x6 -> x0, local copies, waits for them, and re-layouts: 7.02 us -> none  [the longest x4 6.88 us: classify(): padded[tap_row:tap_row + out_rows, tap_col:tap_col + out_cols]]
    sub x2 -> x0, matrix products: 6.71 us -> none  [one_block(): exponent = jnp.exp(scores - highest)]
    ppermute x2 -> x0, starting transfers between devices: 4.84 us -> none  [the longest x1 3.37 us: extended_2(): lax.ppermute(lax.slice_in_dim(block, block.shape[dim] - width, None, axis...]
  transfers between devices with their start and end apart: 6 -> 0, of which waited for: 6 -> 0; matrix products, arithmetic and copies ran while one was open for 2% -> 0% of each run, Pallas kernels for 0% -> 0%
where the time goes in v1:
time: 72.6 us; the launch traced here: 72.3 us
  Pallas kernels  65.7 us (90%)
  local copies, waits for them, and re-layouts  4.19 us (6%)
  between operations  2.39 us (3%)
    pallas_call x1, Pallas kernels, body(): pl.pallas_call(functools.partial(kernel, n), out_shape=(jax.ShapeDtypeStr...  65.7 us
    unnamed x2, local copies, waits for them, and re-layouts  2.86 us

profile of v1, /device:TPU:0, one launch (start us, length us, event | category | flops | bytes accessed | tf_op | source)
XLA Modules:
  0.0 72.3 jit_solution(11274259029911744325)
XLA Ops:
  0.6 1.3 %copy.16.tb_ref = f32[16,1]{1,0:T(8,128)} copy(f32[16,1]{0,1:T(1,128)} %bitcast.8) | data formatting | bytes 128 | tf_op jit(solution)/shard_map/reshape | solution.py:443
  2.0 65.7 %shard_map.148 = (f32[16,8,256]{2,1,0:T(8,128)}, f32[8,256]{1,0:T(8,128)}, f32[1,1]{1,0:T(1,128)}) custom-call(bf16[128,2048]{1,0:T(8,128)(2,1)} %q_ref.1, bf16[128,2048]{1,0:T(8,128)(2,1)} %k_ref.1, bf16[128,2048]{1,0:T(8,128)(2,1)} %v_ref.1, bf16[2048,256]{1,0:T(8,128)(2,1)} %pw_ref.1, f32[1,256]{1,0:T(1,128)} %bitcast.6, bf16[9,256,256]{2,1,0:T(8,128)(2,1)} %cw_ref.1, ...), custom_call_target="tpu_custom_call" | custom-call | tf_op jit(solution)/shard_map/pallas_call | solution.py:397
  67.7 1.6 %copy.20 = f32[16,8,256]{2,1,0:T(8,128)} copy(f32[16,8,256]{2,1,0:T(8,128)} %get-tuple-element.12) | data formatting | bytes 262144
  69.3 1.3 %copy.21 = f32[8,256]{1,0:T(8,128)} copy(f32[8,256]{1,0:T(8,128)} %get-tuple-element.13) | data formatting | bytes 16384

commit v2 on v1

--- a/solution.py
+++ b/solution.py
@@ -47,8 +47,19 @@
     k_ref,
     v_ref,
     pw_ref,
+    gain_in,
+    cw_ref,
+    cb_in,
+    tw_in,
+    tb_in,
+    lab_in,
+    row_in,
+    col_in,
+    up_in,
+    logits_out,
+    losses_out,
+    loss_ref,
     gain_ref,
-    cw_ref,
     cb_ref,
     tw_ref,
     tb_ref,
@@ -58,7 +69,6 @@
     up_ref,
     logits_ref,
     losses_ref,
-    loss_ref,
     qx,
     kx,
     pw,
@@ -82,6 +92,8 @@
     lsend,
     lrecv,
     local,
+    small,
+    results,
 ):
     me = lax.axis_index("seq")
     hpd, keys, dim = kbuf.shape
@@ -103,40 +115,6 @@
 
         lax.fori_loop(0, n - 1, step, 0)
 
-    barrier = pltpu.get_barrier_semaphore()
-    each_peer(
-        lambda d: pl.semaphore_signal(barrier, inc=1, device_id={"seq": d}, device_id_type=MESH)
-    )
-    load_k = pltpu.make_async_copy(k_ref, kx, local.at[0])
-    load_q = pltpu.make_async_copy(q_ref, qx, local.at[1])
-    load_pw = pltpu.make_async_copy(pw_ref, pw, local.at[2])
-    load_cw = pltpu.make_async_copy(cw_ref, cw, local.at[3])
-    load_k.start()
-    load_q.start()
-    own_v = []
-    for h in range(hpd):
-        cols = pl.ds(pl.multiple_of((my_group * hpd + h) * dim, dim), dim)
-        rows = pl.ds(pl.multiple_of(me * tokens, tokens), tokens)
-        copy = pltpu.make_async_copy(v_ref.at[:, cols], vbuf.at[h, rows], local.at[4 + h])
-        copy.start()
-        own_v.append(copy)
-    load_pw.start()
-    load_cw.start()
-
-    turn = []
-    for t in range(3):
-        pieces = []
-        for r in range(strip):
-            pieces.append(row_ref[t, pl.ds(me * strip + r, 1), :] + col_ref[t])
-        turn.append(jnp.concatenate(pieces, axis=0) if strip > 1 else pieces[0])
-
-    def rotate(src, dst, h):
-        for g in range(HEADS // hpd):
-            head = g * hpd + h
-            x = src[:, head * dim : (head + 1) * dim].astype(F32)
-            out = x * turn[0] + pltpu.roll(x, 96, 1) * turn[1] + pltpu.roll(x, 32, 1) * turn[2]
-            dst[head] = out.astype(BF16)
-
     def v_copy(h, d, s):
         head = (d // split) * hpd + h
         return pltpu.make_async_remote_copy(
@@ -148,6 +126,65 @@
             device_id_type=MESH,
         )
 
+    barrier = pltpu.get_barrier_semaphore()
+    each_peer(
+        lambda d: pl.semaphore_signal(barrier, inc=1, device_id={"seq": d}, device_id_type=MESH)
+    )
+    load_k = pltpu.make_async_copy(k_ref, kx, local.at[0])
+    load_q = pltpu.make_async_copy(q_ref, qx, local.at[1])
+    load_pw = pltpu.make_async_copy(pw_ref, pw, local.at[2])
+    load_cw = pltpu.make_async_copy(cw_ref, cw, local.at[3])
+    first = [
+        pltpu.make_async_copy(a, b, small.at[i])
+        for i, (a, b) in enumerate(((row_in, row_ref), (col_in, col_ref)))
+    ]
+    later = [
+        pltpu.make_async_copy(a, b, small.at[i + 2])
+        for i, (a, b) in enumerate(
+            (
+                (gain_in, gain_ref),
+                (cb_in, cb_ref),
+                (tw_in, tw_ref),
+                (tb_in, tb_ref),
+                (lab_in, lab_ref),
+                (up_in, up_ref),
+            )
+        )
+    ]
+    load_k.start()
+    for copy in first:
+        copy.start()
+    load_q.start()
+    own_v = []
+    for h in range(hpd):
+        cols = pl.ds(pl.multiple_of((my_group * hpd + h) * dim, dim), dim)
+        rows = pl.ds(pl.multiple_of(me * tokens, tokens), tokens)
+        copy = pltpu.make_async_copy(v_ref.at[:, cols], vbuf.at[h, rows], local.at[4 + h])
+        copy.start()
+        own_v.append(copy)
+    pl.semaphore_wait(barrier, n - 1)
+    each_peer(lambda d: v_copy(0, d, me).start())
+    load_pw.start()
+    load_cw.start()
+    for copy in later:
+        copy.start()
+    for copy in first:
+        copy.wait()
+
+    turn = []
+    for t in range(3):
+        pieces = []
+        for r in range(strip):
+            pieces.append(row_ref[t, pl.ds(me * strip + r, 1), :] + col_ref[t])
+        turn.append(jnp.concatenate(pieces, axis=0) if strip > 1 else pieces[0])
+
+    def rotate(src, dst, h):
+        for g in range(HEADS // hpd):
+            head = g * hpd + h
+            x = src[:, head * dim : (head + 1) * dim].astype(F32)
+            out = x * turn[0] + pltpu.roll(x, 96, 1) * turn[1] + pltpu.roll(x, 32, 1) * turn[2]
+            dst[head] = out.astype(BF16)
+
     def k_copy(h, d, s):
         return pltpu.make_async_remote_copy(
             src_ref=rk.at[(d // split) * hpd + h],
@@ -170,17 +207,15 @@
         )
 
     load_k.wait()
-    rotate(kx, rk, 0)
-    pl.semaphore_wait(barrier, n - 1)
     for h in range(hpd):
-        if h > 0:
-            rotate(kx, rk, h)
+        rotate(kx, rk, h)
         each_peer(lambda d: k_copy(h, d, me).start())
         if h == 0:
             load_q.wait()
         rotate(qx, rq, h)
         each_peer(lambda d: q_copy(h, d, me).start())
-        each_peer(lambda d: v_copy(h, d, me).start())
+        if h + 1 < hpd:
+            each_peer(lambda d: v_copy(h + 1, d, me).start())
         head = my_group * hpd + h
         kbuf[h, pl.ds(pl.multiple_of(me * tokens, tokens), tokens), :] = rk[head]
         qbuf[h, pl.ds(pl.multiple_of(me * part, part), part), :] = rq[
@@ -207,10 +242,10 @@
     factor = dim ** (-0.5) * math.log2(math.e)
 
     for h in range(hpd):
+        own_v[h].wait()
+        each_peer(lambda s: v_copy(h, s, s).wait_recv())
         each_peer(lambda s: k_copy(h, s, s).wait_recv())
         each_peer(lambda s: q_copy(h, s, s).wait_recv())
-        own_v[h].wait()
-        each_peer(lambda s: v_copy(h, s, s).wait_recv())
 
         def attend(i, carry):
             j = lax.rem(me // in_block + blocks // 2 + i, blocks)
@@ -241,6 +276,9 @@
         ] = obuf[h, pl.ds(pl.multiple_of(me * part, part), part), :]
 
     load_pw.wait()
+    load_cw.wait()
+    for copy in later:
+        copy.wait()
     for h in range(hpd):
         each_peer(lambda s: o_copy(h, s, s).wait_recv())
     features = jnp.dot(mix[...], pw[...], preferred_element_type=F32)
@@ -271,7 +309,11 @@
     )
     to_up.start()
     to_down.start()
-    load_cw.wait()
+    for h in range(hpd):
+        each_peer(lambda d: v_copy(h, d, me).wait_send())
+        each_peer(lambda d: k_copy(h, d, me).wait_send())
+        each_peer(lambda d: q_copy(h, d, me).wait_send())
+        each_peer(lambda d: o_copy(h, d, me).wait_send())
     to_up.wait()
     to_down.wait()
 
@@ -299,7 +341,7 @@
 
     width = cols * UPSCALE
     lane = lax.broadcasted_iota(jnp.int32, (1, width), 1)
-    classes = tb_ref.shape[0]
+    classes = tb_ref.shape[1]
     rows_of = []
     for r in range(strip + 2):
         wide = jnp.dot(
@@ -317,7 +359,9 @@
                 for t in range(3)
             ]
         )
-    bias = tb_ref[...]
+    ids = lax.broadcasted_iota(jnp.int32, (classes, classes), 0)
+    diagonal = ids == lax.broadcasted_iota(jnp.int32, (classes, classes), 1)
+    bias = jnp.sum(jnp.where(diagonal, tb_ref[...], 0.0), axis=1, keepdims=True)
     ids = lax.broadcasted_iota(jnp.int32, (classes, width), 0)
     running = jnp.zeros((1, width), F32)
     for r in range(strip):
@@ -356,16 +400,19 @@
         )
 
     each_peer(lambda d: l_copy(d, me).start())
+    write = [
+        pltpu.make_async_copy(logits_ref, logits_out, results.at[0]),
+        pltpu.make_async_copy(losses_ref, losses_out, results.at[1]),
+    ]
+    for copy in write:
+        copy.start()
     sums[me] = part_sum[...]
-    for h in range(hpd):
-        each_peer(lambda d: v_copy(h, d, me).wait_send())
-        each_peer(lambda d: k_copy(h, d, me).wait_send())
-        each_peer(lambda d: q_copy(h, d, me).wait_send())
-        each_peer(lambda d: o_copy(h, d, me).wait_send())
     each_peer(lambda s: l_copy(s, s).wait_recv())
     each_peer(lambda d: l_copy(d, me).wait_send())
     pixels = n * strip * UPSCALE * width
     loss_ref[...] = jnp.sum(sums[...], axis=0)[0:1, 0:1] / pixels
+    for copy in write:
+        copy.wait()
 
 
 def body(
@@ -401,9 +448,19 @@
             jax.ShapeDtypeStruct(labels.shape, F32),
             jax.ShapeDtypeStruct((1, 1), F32),
         ),
-        in_specs=[hbm, hbm, hbm, hbm, vmem, hbm] + [vmem] * 7,
-        out_specs=(vmem, vmem, vmem),
+        in_specs=[hbm] * 13,
+        out_specs=(hbm, hbm, vmem),
         scratch_shapes=[
+            pltpu.VMEM((1, channels), F32),
+            pltpu.VMEM((1, channels), F32),
+            pltpu.VMEM((9 * classes, channels), BF16),
+            pltpu.VMEM((1, classes), F32),
+            pltpu.VMEM(labels.shape, jnp.int32),
+            pltpu.VMEM(row_table.shape, F32),
+            pltpu.VMEM(col_table.shape, F32),
+            pltpu.VMEM(spread.shape, BF16),
+            pltpu.VMEM((classes,) + labels.shape, F32),
+            pltpu.VMEM(labels.shape, F32),
             pltpu.VMEM((tokens, HEADS * HEAD_DIM), BF16),
             pltpu.VMEM((tokens, HEADS * HEAD_DIM), BF16),
             pltpu.VMEM(proj_weight.shape, BF16),
@@ -427,6 +484,8 @@
             dma((n,)),
             dma((n,)),
             dma((4 + hpd,)),
+            dma((8,)),
+            dma((2,)),
         ],
         compiler_params=pltpu.CompilerParams(
             collective_id=0, has_side_effects=True, vmem_limit_bytes=56 * 1024 * 1024
@@ -440,7 +499,7 @@
         conv_weight,
         conv_bias.reshape(1, -1),
         class_weight.reshape(-1, class_weight.shape[2]),
-        class_bias.reshape(-1, 1),
+        class_bias.reshape(1, -1),
         labels,
         jnp.asarray(row_table),
         jnp.asarray(col_table),

time: 72.6 us -> 70.6 us (0.972)
  local copies, waits for them, and re-layouts: 4.19 us -> 2.86 us
    reshape x1 -> x0, local copies, waits for them, and re-layouts: 1.33 us -> none  [body(): class_bias.reshape(-1, 1)]
where the time goes in v2:
time: 70.6 us; the launch traced here: 70.4 us
  Pallas kernels  65.1 us (92%)
  local copies, waits for them, and re-layouts  2.86 us (4%)
  between operations  2.4 us (3%)
    pallas_call x1, Pallas kernels, body(): pl.pallas_call(functools.partial(kernel, n), out_shape=(jax.ShapeDtypeStr...  65.1 us
    unnamed x2, local copies, waits for them, and re-layouts  2.86 us

profile of v2, /device:TPU:0, one launch (start us, length us, event | category | flops | bytes accessed | tf_op | source)
XLA Modules:
  0.0 70.4 jit_solution(6176557978448398913)
XLA Ops:
  0.6 65.1 %shard_map.148 = (f32[16,8,256]{2,1,0:T(8,128)}, f32[8,256]{1,0:T(8,128)}, f32[1,1]{1,0:T(1,128)}) custom-call(bf16[128,2048]{1,0:T(8,128)(2,1)} %q_ref.1, bf16[128,2048]{1,0:T(8,128)(2,1)} %k_ref.1, bf16[128,2048]{1,0:T(8,128)(2,1)} %v_ref.1, bf16[2048,256]{1,0:T(8,128)(2,1)} %pw_ref.1, f32[1,256]{1,0:T(1,128)} %bitcast.6, bf16[9,256,256]{2,1,0:T(8,128)(2,1)} %cw_ref.1, ...), custom_call_target="tpu_custom_call" | custom-call | tf_op jit(solution)/shard_map/pallas_call | solution.py:444
  65.7 1.6 %copy.19 = f32[16,8,256]{2,1,0:T(8,128)} copy(f32[16,8,256]{2,1,0:T(8,128)} %get-tuple-element.12) | data formatting | bytes 262144
  67.3 1.3 %copy.20 = f32[8,256]{1,0:T(8,128)} copy(f32[8,256]{1,0:T(8,128)} %get-tuple-element.13) | data formatting | bytes 16384

commit v3 on v2

--- a/solution.py
+++ b/solution.py
@@ -132,7 +132,9 @@
     )
     load_k = pltpu.make_async_copy(k_ref, kx, local.at[0])
     load_q = pltpu.make_async_copy(q_ref, qx, local.at[1])
-    load_pw = pltpu.make_async_copy(pw_ref, pw, local.at[2])
+    load_pw = [
+        pltpu.make_async_copy(pw_ref.at[:, h], pw.at[h], local.at[4 + hpd + h]) for h in range(hpd)
+    ]
     load_cw = pltpu.make_async_copy(cw_ref, cw, local.at[3])
     first = [
         pltpu.make_async_copy(a, b, small.at[i])
@@ -164,7 +166,8 @@
         own_v.append(copy)
     pl.semaphore_wait(barrier, n - 1)
     each_peer(lambda d: v_copy(0, d, me).start())
-    load_pw.start()
+    for copy in load_pw:
+        copy.start()
     load_cw.start()
     for copy in later:
         copy.start()
@@ -223,12 +226,12 @@
         ]
 
     def o_copy(h, d, s):
-        head = (s // split) * hpd + h
         return pltpu.make_async_remote_copy(
             src_ref=obuf.at[h, pl.ds(pl.multiple_of(d * part, part), part)],
             dst_ref=mix.at[
+                h,
                 pl.ds(pl.multiple_of(lax.rem(s, split) * part, part), part),
-                pl.ds(pl.multiple_of(head * dim, dim), dim),
+                pl.ds(pl.multiple_of((s // split) * dim, dim), dim),
             ],
             send_sem=osend.at[h, d],
             recv_sem=orecv.at[h, s],
@@ -245,10 +248,17 @@
         own_v[h].wait()
         each_peer(lambda s: v_copy(h, s, s).wait_recv())
         each_peer(lambda s: k_copy(h, s, s).wait_recv())
-        each_peer(lambda s: q_copy(h, s, s).wait_recv())
 
         def attend(i, carry):
-            j = lax.rem(me // in_block + blocks // 2 + i, blocks)
+            shift = blocks // 2 + ((i + 1) // 2) * (1 - 2 * lax.rem(i, 2))
+            j = lax.rem(me // in_block + shift, blocks)
+            for u in range(in_block):
+                s = j * in_block + u
+
+                @pl.when(s != me)
+                def _():
+                    q_copy(h, s, s).wait_recv()
+
             rows = pl.ds(pl.multiple_of(j * block, block), block)
             scores = lax.dot_general(
                 qbuf[h, rows, :], kbuf[h], (((1,), (1,)), ((), ())), preferred_element_type=F32
@@ -269,19 +279,23 @@
             return carry
 
         lax.fori_loop(0, blocks, attend, 0, unroll=blocks <= 4)
-        head = my_group * hpd + h
         mix[
+            h,
             pl.ds(pl.multiple_of(my_part * part, part), part),
-            pl.ds(pl.multiple_of(head * dim, dim), dim),
+            pl.ds(pl.multiple_of(my_group * dim, dim), dim),
         ] = obuf[h, pl.ds(pl.multiple_of(me * part, part), part), :]
 
-    load_pw.wait()
+    for copy in load_pw:
+        copy.wait()
     load_cw.wait()
     for copy in later:
         copy.wait()
+    features = None
     for h in range(hpd):
         each_peer(lambda s: o_copy(h, s, s).wait_recv())
-    features = jnp.dot(mix[...], pw[...], preferred_element_type=F32)
+        weight = pw[h].reshape(-1, pw.shape[3])
+        term = jnp.dot(mix[h], weight, preferred_element_type=F32)
+        features = term if features is None else features + term
     center = jnp.mean(features, axis=-1, keepdims=True)
     shifted = features - center
     spread = jnp.mean(shifted * shifted, axis=-1, keepdims=True)
@@ -307,15 +321,31 @@
         device_id={"seq": down},
         device_id_type=MESH,
     )
-    to_up.start()
-    to_down.start()
+
+    @pl.when(me < n - 1)
+    def _():
+        to_up.start()
+
+    @pl.when(me > 0)
+    def _():
+        to_down.start()
+
     for h in range(hpd):
         each_peer(lambda d: v_copy(h, d, me).wait_send())
         each_peer(lambda d: k_copy(h, d, me).wait_send())
         each_peer(lambda d: q_copy(h, d, me).wait_send())
         each_peer(lambda d: o_copy(h, d, me).wait_send())
-    to_up.wait()
-    to_down.wait()
+
+    @pl.when(me < n - 1)
+    def _():
+        to_up.wait_send()
+        to_down.wait_recv()
+
+    @pl.when(me > 0)
+    def _():
+        to_down.wait_send()
+        to_up.wait_recv()
+
 
     place = lax.broadcasted_iota(jnp.int32, (tokens + 2 * halo, 1), 0)
     grid_row = place // cols + (me * strip - 2)
@@ -463,7 +493,7 @@
             pltpu.VMEM(labels.shape, F32),
             pltpu.VMEM((tokens, HEADS * HEAD_DIM), BF16),
             pltpu.VMEM((tokens, HEADS * HEAD_DIM), BF16),
-            pltpu.VMEM(proj_weight.shape, BF16),
+            pltpu.VMEM((hpd, HEADS // hpd, HEAD_DIM, channels), BF16),
             pltpu.VMEM(conv_weight.shape, BF16),
             pltpu.VMEM((HEADS, tokens, HEAD_DIM), BF16),
             pltpu.VMEM((HEADS, tokens, HEAD_DIM), BF16),
@@ -471,7 +501,7 @@
             pltpu.VMEM((hpd, n * tokens, HEAD_DIM), BF16),
             pltpu.VMEM((hpd, n * tokens, HEAD_DIM), BF16),
             pltpu.VMEM((hpd, n * part, HEAD_DIM), BF16),
-            pltpu.VMEM((tokens, HEADS * HEAD_DIM), BF16),
+            pltpu.VMEM((hpd, tokens, HEADS // hpd * HEAD_DIM), BF16),
             pltpu.VMEM((tokens + 4 * GRID_COLS, channels), BF16),
             pltpu.VMEM((8, 128), F32),
             pltpu.VMEM((n, 8, 128), F32),
@@ -483,7 +513,7 @@
             dma((2,)),
             dma((n,)),
             dma((n,)),
-            dma((4 + hpd,)),
+            dma((4 + 2 * hpd,)),
             dma((8,)),
             dma((2,)),
         ],
@@ -494,7 +524,7 @@
         queries,
         keys,
         values,
-        proj_weight,
+        proj_weight.reshape(HEADS // hpd, hpd, HEAD_DIM, channels),
         norm_gain.reshape(1, -1),
         conv_weight,
         conv_bias.reshape(1, -1),

time: 70.6 us -> 69.8 us (0.989)
  Pallas kernels: 65.1 us -> 64.3 us
    pallas_call x1, Pallas kernels: 65.1 us -> 64.3 us  [body(): pl.pallas_call(functools.partial(kernel, n), out_shape=(jax.ShapeDtypeStr...]
where the time goes in v3:
time: 69.8 us; the launch traced here: 69.6 us
  Pallas kernels  64.3 us (92%)
  local copies, waits for them, and re-layouts  2.86 us (4%)
  between operations  2.4 us (3%)
    pallas_call x1, Pallas kernels, body(): pl.pallas_call(functools.partial(kernel, n), out_shape=(jax.ShapeDtypeStr...  64.3 us
    unnamed x2, local copies, waits for them, and re-layouts  2.86 us

profile of v3, /device:TPU:0, one launch (start us, length us, event | category | flops | bytes accessed | tf_op | source)
XLA Modules:
  0.0 69.6 jit_solution(3108408822595329615)
XLA Ops:
  0.6 64.3 %shard_map.148 = (f32[16,8,256]{2,1,0:T(8,128)}, f32[8,256]{1,0:T(8,128)}, f32[1,1]{1,0:T(1,128)}) custom-call(bf16[128,2048]{1,0:T(8,128)(2,1)} %q_ref.1, bf16[128,2048]{1,0:T(8,128)(2,1)} %k_ref.1, bf16[128,2048]{1,0:T(8,128)(2,1)} %v_ref.1, bf16[8,2,128,256]{3,2,1,0:T(8,128)(2,1)} %bitcast.6, f32[1,256]{1,0:T(1,128)} %bitcast.8, ...), custom_call_target="tpu_custom_call" | custom-call | tf_op jit(solution)/shard_map/pallas_call | solution.py:474
  64.9 1.6 %copy.19 = f32[16,8,256]{2,1,0:T(8,128)} copy(f32[16,8,256]{2,1,0:T(8,128)} %get-tuple-element.12) | data formatting | bytes 262144
  66.5 1.3 %copy.20 = f32[8,256]{1,0:T(8,128)} copy(f32[8,256]{1,0:T(8,128)} %get-tuple-element.13) | data formatting | bytes 16384

commit v4 on v3

--- a/solution.py
+++ b/solution.py
@@ -478,7 +478,7 @@
             jax.ShapeDtypeStruct(labels.shape, F32),
             jax.ShapeDtypeStruct((1, 1), F32),
         ),
-        in_specs=[hbm] * 13,
+        in_specs=[pl.BlockSpec(memory_space=pltpu.HBM)] * 13,
         out_specs=(hbm, hbm, vmem),
         scratch_shapes=[
             pltpu.VMEM((1, channels), F32),
@@ -518,7 +518,7 @@
             dma((2,)),
         ],
         compiler_params=pltpu.CompilerParams(
-            collective_id=0, has_side_effects=True, vmem_limit_bytes=56 * 1024 * 1024
+            collective_id=0, has_side_effects=True, vmem_limit_bytes=24 * 1024 * 1024
         ),
     )(
         queries,

time: 69.8 us -> 79.7 us (1.14)
  local copies, waits for them, and re-layouts: 2.86 us -> 12.9 us
    unnamed x2 -> x28, local copies, waits for them, and re-layouts: 2.86 us -> 12.9 us
where the time goes in v4:
time: 79.7 us; the launch traced here: 79.1 us
  Pallas kernels  63.8 us (80%)
  local copies, waits for them, and re-layouts  12.9 us (16%)
  between operations  2.35 us (3%)
    pallas_call x1, Pallas kernels, body(): pl.pallas_call(functools.partial(kernel, n), out_shape=(jax.ShapeDtypeStr...  63.8 us
    unnamed x28, local copies, waits for them, and re-layouts  12.9 us

profile of v4, /device:TPU:0, one launch (start us, length us, event | category | flops | bytes accessed | tf_op | source)
XLA Modules:
  0.0 79.1 jit_solution(16317170905063392123)
XLA Ops:
  0.6 0.0 copy-start
  0.6 1.3 %copy-done = bf16[9,256,256]{2,1,0:T(8,128)(2,1)S(1)} copy-done((bf16[9,256,256]{2,1,0:T(8,128)(2,1)S(1)}, bf16[9,256,256]{2,1,0:T(8,128)(2,1)}, u32[]{:S(2)}) %copy-start) | copy-done | bytes 1179672
  1.9 0.0 copy-start.1
  1.9 1.2 %copy-done.1 = bf16[2048,256]{1,0:T(8,128)(2,1)S(1)} copy-done((bf16[2048,256]{1,0:T(8,128)(2,1)S(1)}, bf16[2048,256]{1,0:T(8,128)(2,1)}, u32[]{:S(2)}) %copy-start.1) | copy-done | bytes 1048600
  3.1 0.0 copy-start.2
  3.1 1.0 %copy-done.2 = bf16[128,2048]{1,0:T(8,128)(2,1)S(1)} copy-done((bf16[128,2048]{1,0:T(8,128)(2,1)S(1)}, bf16[128,2048]{1,0:T(8,128)(2,1)}, u32[]{:S(2)}) %copy-start.2) | copy-done | bytes 524312
  4.2 0.0 copy-start.3
  4.2 1.0 %copy-done.3 = bf16[128,2048]{1,0:T(8,128)(2,1)S(1)} copy-done((bf16[128,2048]{1,0:T(8,128)(2,1)S(1)}, bf16[128,2048]{1,0:T(8,128)(2,1)}, u32[]{:S(2)}) %copy-start.3) | copy-done | bytes 524312
  5.2 0.0 copy-start.4
  5.2 1.0 %copy-done.4 = bf16[128,2048]{1,0:T(8,128)(2,1)S(1)} copy-done((bf16[128,2048]{1,0:T(8,128)(2,1)S(1)}, bf16[128,2048]{1,0:T(8,128)(2,1)}, u32[]{:S(2)}) %copy-start.4) | copy-done | bytes 524312
  6.3 0.0 copy-start.5
  6.3 0.9 %copy-done.5 = f32[3,64,128]{2,1,0:T(8,128)S(1)} copy-done((f32[3,64,128]{2,1,0:T(8,128)S(1)}, f32[3,64,128]{2,1,0:T(8,128)}, u32[]{:S(2)}) %copy-start.5) | copy-done | bytes 98328
  7.2 0.0 copy-start.6
  7.2 0.9 %copy-done.6 = bf16[9,16,256]{2,1,0:T(8,128)(2,1)S(1)} copy-done((bf16[9,16,256]{2,1,0:T(8,128)(2,1)S(1)}, bf16[9,16,256]{2,1,0:T(8,128)(2,1)}, u32[]{:S(2)}) %copy-start.6) | copy-done | bytes 73752
  8.0 0.0 copy-start.7
  8.0 0.8 %copy-done.7 = bf16[256,64]{1,0:T(8,128)(2,1)S(1)} copy-done((bf16[256,64]{1,0:T(8,128)(2,1)S(1)}, bf16[256,64]{1,0:T(8,128)(2,1)}, u32[]{:S(2)}) %copy-start.7) | copy-done | bytes 32792
  8.9 0.0 copy-start.8
  8.9 0.7 copy-done.8
  9.6 0.0 copy-start.9
  9.6 0.7 copy-done.9
  10.3 0.0 copy-start.10
  10.3 0.7 copy-done.10
  11.0 0.0 copy-start.11
  11.0 0.7 copy-done.11
  11.7 0.0 copy-start.12
  11.7 0.7 copy-done.12
  12.3 63.8 %shard_map.148 = (f32[16,8,256]{2,1,0:T(8,128)S(1)}, f32[8,256]{1,0:T(8,128)S(1)}, f32[1,1]{1,0:T(1,128)}) custom-call(bf16[128,2048]{1,0:T(8,128)(2,1)S(1)} %copy-done.2, bf16[128,2048]{1,0:T(8,128)(2,1)S(1)} %copy-done.3, bf16[128,2048]{1,0:T(8,128)(2,1)S(1)} %copy-done.4, bf16[8,2,128,256]{3,2,1,0:T(8,128)(2,1)S(1)} %bitcast.6, f32[1,256]{1,0:T(1,128)S(1)} %bitcast.8, ...), custom_call_target="tpu_custom_call" | custom-call | tf_op jit(solution)/shard_map/pallas_call | solution.py:474
  76.2 0.7 copy.19
  76.8 0.6 copy.20
Async XLA Ops:
  0.6 1.3 %copy-start = (bf16[9,256,256]{2,1,0:T(8,128)(2,1)S(1)}, bf16[9,256,256]{2,1,0:T(8,128)(2,1)}, u32[]{:S(2)}) copy-start(bf16[9,256,256]{2,1,0:T(8,128)(2,1)} %cw_ref.1) | copy-start | bytes 3538948
  1.9 1.2 %copy-start.1 = (bf16[2048,256]{1,0:T(8,128)(2,1)S(1)}, bf16[2048,256]{1,0:T(8,128)(2,1)}, u32[]{:S(2)}) copy-start(bf16[2048,256]{1,0:T(8,128)(2,1)} %param.16) | copy-start | bytes 3145732
  3.1 1.0 %copy-start.2 = (bf16[128,2048]{1,0:T(8,128)(2,1)S(1)}, bf16[128,2048]{1,0:T(8,128)(2,1)}, u32[]{:S(2)}) copy-start(bf16[128,2048]{1,0:T(8,128)(2,1)} %q_ref.1) | copy-start | bytes 1572868
  4.2 1.0 %copy-start.3 = (bf16[128,2048]{1,0:T(8,128)(2,1)S(1)}, bf16[128,2048]{1,0:T(8,128)(2,1)}, u32[]{:S(2)}) copy-start(bf16[128,2048]{1,0:T(8,128)(2,1)} %k_ref.1) | copy-start | bytes 1572868
  5.2 1.0 %copy-start.4 = (bf16[128,2048]{1,0:T(8,128)(2,1)S(1)}, bf16[128,2048]{1,0:T(8,128)(2,1)}, u32[]{:S(2)}) copy-start(bf16[128,2048]{1,0:T(8,128)(2,1)} %v_ref.1) | copy-start | bytes 1572868
  6.3 0.9 %copy-start.5 = (f32[3,64,128]{2,1,0:T(8,128)S(1)}, f32[3,64,128]{2,1,0:T(8,128)}, u32[]{:S(2)}) copy-start(f32[3,64,128]{2,1,0:T(8,128)} %constant.7.clone.col_in) | copy-start | bytes 294916
  7.2 0.9 %copy-start.6 = (bf16[9,16,256]{2,1,0:T(8,128)(2,1)S(1)}, bf16[9,16,256]{2,1,0:T(8,128)(2,1)}, u32[]{:S(2)}) copy-start(bf16[9,16,256]{2,1,0:T(8,128)(2,1)} %param.20) | copy-start | bytes 221188
  8.0 0.8 %copy-start.7 = (bf16[256,64]{1,0:T(8,128)(2,1)S(1)}, bf16[256,64]{1,0:T(8,128)(2,1)}, u32[]{:S(2)}) copy-start(bf16[256,64]{1,0:T(8,128)(2,1)} %constant.8.clone.up_in) | copy-start | bytes 98308
  8.9 0.7 copy-start.8
  9.6 0.7 copy-start.9
  10.3 0.7 copy-start.10
  11.0 0.7 copy-start.11
  11.7 0.7 copy-start.12
